TPU v7x, 32 devices: a whole 2x2x4 slice. The times are simulated.
32 devices in a mesh: chan: 8 (over z, y), row: 4 (over x, core).
Axes of the slice: x: 2, y: 2, z: 4, core: 2. Of those that a mesh axis runs over, the one named last changes fastest.
Arguments:
- eta_pp: float32 [8, 1024, 1024], P('chan', 'row'), as said below
- ham_pp: float32 [8, 1024, 1024], P('chan', 'row'), as said below
- block_size: int32 [8], P('chan'), may hold values from 128 to 1024, as said below
- pp_occupancy: float32 [8, 1024], P('chan'), may hold values from -1 to 1
- ph_occupancy: float32 [8, 1024], P('chan'), may hold values from -1 to 1
- coupling: float32 [8, 8, 128, 128], P('chan'), may hold values from -0.5 to 0.5
- channel_weight: float32 [8], P('chan'), may hold values from 0.02 to 1
- orbit_of: int32 [8, 1024], P('chan', 'row'), may hold values from 0 to 239
- tile_target: int32 [8, 4, 256], P('chan', 'row'), may hold values from 0 to 7, as said below
- tile_source: int32 [8, 4, 256], P('chan', 'row'), may hold values from 0 to 7, as said below
Outputs:
- comm: float32 [8, 1024, 1024], P('chan', 'row')
- onebody: float32 [240], replicated
Inputs may be any that keep to these rules, and one draw needn't show every extreme that they name: Each block of eta_pp is antisymmetric: eta_pp[c, a, b] = -eta_pp[c, b, a]. Each block of ham_pp is symmetric: ham_pp[c, a, b] = ham_pp[c, b, a]. `block_size`: some channel has order 1024. Within each row group, at most 48 tiles of one block go to one block, and in every draw and row group every block sends exactly 48 tiles to some block. For every row group r and blocks c, p, the count of t with tile_target[c, r, t] = p equals the count of q with tile_source[p, r, q] = c. `tile_source`: agrees with tile_target as stated there.
All inputs are finite; a program needn't handle non-finite values.
Results may differ from a plain program's by a relative error of at most 0.000078.
Values sent between devices are 32-bit elements; how exact they have to be, the bound alone decides.
A program may use at most 64 MiB of HBM per device.

v0:
```python
import math

import jax
import jax.numpy as jnp
from jax import lax
from jax.sharding import PartitionSpec as P

TW = 128
TR = 8
NORB = 240


precise = lax.Precision.HIGHEST


def cut_tiles(matrix):
    row_count, col_count = matrix.shape
    shaped = matrix.reshape(row_count // TR, TR, col_count // TW, TW).transpose(0, 2, 1, 3)
    return shaped.reshape(-1, TR, TW)


def join_tiles(tile_set, row_count, col_count):
    shaped = tile_set.reshape(row_count // TR, col_count // TW, TR, TW).transpose(0, 2, 1, 3)
    return shaped.reshape(row_count, col_count)


def group_rank(labels):
    length = labels.shape[0]
    position = jnp.arange(length, dtype=jnp.int32)
    same_label = labels[:, None] == labels[None, :]
    before = position[None, :] < position[:, None]
    return jnp.sum((same_label & before).astype(jnp.int32), axis=1)


def pack_slots(tile_set, slot_of, slot_total):
    length = tile_set.shape[0]
    matches = slot_of[None, :] == jnp.arange(slot_total, dtype=jnp.int32)[:, None]
    source = jnp.sum(jnp.where(matches, jnp.arange(length, dtype=jnp.int32)[None, :], 0), axis=1)
    filled = jnp.any(matches, axis=1)
    picked = jnp.take(tile_set, source, axis=0)
    mask_shape = (slot_total,) + (1,) * (tile_set.ndim - 1)
    return jnp.where(filled.reshape(mask_shape), picked, jnp.zeros_like(picked))


def mix_tiles(tile_set, mixers, transpose):
    length = tile_set.shape[0]
    band_count = mixers.shape[0]
    arranged = tile_set.reshape(length // band_count, band_count, TR, TW)
    pattern = "gbij,bkj->gbik" if transpose else "gbij,bjk->gbik"
    mixed = jnp.einsum(pattern, arranged, mixers, precision=precise)
    return mixed.reshape(length, TR, TW)


def per_device(
    eta_pp,
    ham_pp,
    block_size,
    pp_occupancy,
    ph_occupancy,
    coupling,
    channel_weight,
    orbit_of,
    tile_target,
    tile_source,
):
    row_count = eta_pp.shape[1]
    col_count = eta_pp.shape[2]
    channels = lax.axis_size("chan")
    row_start = lax.axis_index("row") * row_count
    row_ids = row_start + jnp.arange(row_count, dtype=jnp.int32)
    col_ids = jnp.arange(col_count, dtype=jnp.int32)
    live_rows = (row_ids < block_size[0]).astype(jnp.float32)
    live_cols = (col_ids < block_size[0]).astype(jnp.float32)
    outer_mask = live_rows[:, None] * live_cols[None, :]
    eta_rows = eta_pp[0] * outer_mask
    ham_rows = ham_pp[0] * outer_mask
    weights = pp_occupancy[0]
    occupancy = ph_occupancy[0]
    mixers = coupling[0]
    tiles_count = row_count // TR * (col_count // TW)
    capacity = max(2, 3 * tiles_count // (2 * channels))
    slot_total = capacity * channels
    targets = tile_target[0, 0]
    send_slot = targets * capacity + group_rank(targets)
    sources = tile_source[0, 0]
    recv_slot = sources * capacity + group_rank(sources)
    eta_arrived = lax.all_to_all(
        pack_slots(cut_tiles(eta_rows), send_slot, slot_total),
        "chan",
        split_axis=0,
        concat_axis=0,
        tiled=True,
    )
    ham_arrived = lax.all_to_all(
        pack_slots(cut_tiles(ham_rows), send_slot, slot_total),
        "chan",
        split_axis=0,
        concat_axis=0,
        tiled=True,
    )
    eta_in = jnp.take(eta_arrived, recv_slot, axis=0)
    ham_in = jnp.take(ham_arrived, recv_slot, axis=0)
    ph_eta = join_tiles(mix_tiles(eta_in, mixers, False), row_count, col_count)
    ph_ham = join_tiles(mix_tiles(ham_in, mixers, False), row_count, col_count)

    def scaled_columns(matrix, factors):
        return matrix * factors[None, :]

    eta_part = scaled_columns(eta_rows, weights)
    ham_part = scaled_columns(ham_rows, weights)
    gained = jnp.dot(
        eta_part,
        lax.all_gather(ham_rows, "row", axis=0, tiled=True),
        precision=precise,
        preferred_element_type=jnp.float32,
    )
    lost = jnp.dot(
        ham_part,
        lax.all_gather(eta_rows, "row", axis=0, tiled=True),
        precision=precise,
        preferred_element_type=jnp.float32,
    )
    ladder = gained - lost
    left_part = scaled_columns(ph_eta, occupancy)
    product = jnp.dot(
        left_part,
        lax.all_gather(ph_ham, "row", axis=0, tiled=True),
        precision=precise,
        preferred_element_type=jnp.float32,
    )
    back_tiles = mix_tiles(cut_tiles(product), mixers, True)
    returned = lax.all_to_all(
        pack_slots(back_tiles, recv_slot, slot_total),
        "chan",
        split_axis=0,
        concat_axis=0,
        tiled=True,
    )
    back_rows = join_tiles(jnp.take(returned, send_slot, axis=0), row_count, col_count)
    mirrored = lax.all_to_all(back_rows, "row", split_axis=1, concat_axis=0, tiled=True).T
    combined = ladder + back_rows + mirrored
    comm_rows = combined * outer_mask
    on_diagonal = (col_ids[None, :] == row_ids[:, None]).astype(jnp.float32)
    diagonal = jnp.sum(comm_rows * on_diagonal, axis=1)
    terms = channel_weight[0] * diagonal
    orbit_table = (orbit_of[0][:, None] == jnp.arange(NORB, dtype=jnp.int32)[None, :]).astype(
        jnp.float32
    )
    partial_value = jnp.dot(
        terms, orbit_table, precision=precise, preferred_element_type=jnp.float32
    )
    gathered_sum = lax.psum(partial_value, ("chan", "row"))
    scale = math.sqrt(NORB / (channels * col_count))
    return (comm_rows[None], gathered_sum * scale)


def solution(mesh):
    return jax.shard_map(
        per_device,
        mesh=mesh,
        in_specs=(
            P("chan", "row", None),
            P("chan", "row", None),
            P("chan"),
            P("chan", None),
            P("chan", None),
            P("chan", None, None, None),
            P("chan"),
            P("chan", "row"),
            P("chan", "row", None),
            P("chan", "row", None),
        ),
        out_specs=(P("chan", "row", None), P()),
        check_vma=False,
    )
```

profile of v0, /device:TPU:0, one launch (start us, length us, event | category | flops | bytes accessed | tf_op | source)
XLA Modules:
  0.0 290.1 jit_solution(1672933856137469680)
XLA Ops:
  7.2 0.9 convert_reduce_fusion
  8.1 0.7 compare_and_fusion
  8.8 0.1 select_reduce_fusion.2
  9.0 0.2 fusion.13
  9.8 1.7 multiply_multiply_fusion.3
  11.6 2.5 gather_fusion
  14.1 2.5 gather_fusion.2
  16.6 4.5 %select_select_fusion.1 = (f32[384,8,128]{2,1,0:T(8,128)}, f32[384,8,128]{2,1,0:T(8,128)S(1)}) fusion(f32[384,8,128]{2,1,0:T(8,128)} %gather_fusion.2, pred[384]{0:T(512)(128)(4,1)S(1)} %compare_and_fusion.3, pred[384]{0:T(512)(128)(4,1)S(1)} %fusion.13, f32[384,8,128]{2,1,0:T(8,128)S(1)} %copy-done.2), kind=kLoop, calls=%fused_computation.10 | loop fusion | flops 1572864 | bytes 6292224 | tf_op jit(solution)/shard_map/jit(_where)/select_n | solution.py:42
  21.1 44.2 %all_to_all.34 = f32[384,8,128]{2,1,0:T(8,128)} all-to-all(f32[384,8,128]{2,1,0:T(8,128)S(1)} %get-tuple-element.13), channel_id=1, replica_groups=mesh['chan'=8,'row'=4] {'chan'}, dimensions={0} | all-to-all | bytes 3145728 | tf_op jit(solution)/shard_map/all_to_all | solution.py:87
  65.3 3.7 %all-to-all-start.1 = ((f32[384,8,128]{2,1,0:T(8,128)}), f32[384,8,128]{2,1,0:T(8,128)S(1)}, u32[]{:S(2)}, u32[]{:S(2)}) async-start(f32[384,8,128]{2,1,0:T(8,128)} %get-tuple-element.12), calls=%async_computation.1 | async-start | bytes 3145728 | tf_op jit(solution)/shard_map/all_to_all | solution.py:94
  69.1 0.2 convert_reduce_fusion.1
  69.3 3.2 %gather_fusion.1 = f32[256,8,128]{2,1,0:T(8,128)} fusion(f32[384,8,128]{2,1,0:T(8,128)} %all_to_all.34, s32[1024]{0:T(1024)S(1)} %pad_clamp_fusion.2), kind=kCustom, calls=%fused_computation.1.clone | custom fusion | bytes 2098176 | tf_op jit(solution)/shard_map/jit(_take)/gather | solution.py:101
  72.5 33.2 %all-to-all-done.1 = f32[384,8,128]{2,1,0:T(8,128)S(1)} async-done(((f32[384,8,128]{2,1,0:T(8,128)}), f32[384,8,128]{2,1,0:T(8,128)S(1)}, u32[]{:S(2)}, u32[]{:S(2)}) %all-to-all-start.1) | async-done | bytes 1572896 | tf_op jit(solution)/shard_map/all_to_all | solution.py:94
  105.7 2.0 gather_fusion.3
  107.7 1.9 broadcast_select_fusion.1
  109.6 1.1 convolution_bitcast_fusion.2
  110.6 0.6 copy.52
  111.3 1.2 copy.50
  112.6 0.1 copy-done.1
  112.7 2.8 multiply_multiply_fusion.2
  115.5 0.2 all-gather.6.cloned.1.call-start
  115.8 0.5 all-gather.6.cloned.1.call-update
  116.3 0.1 select_reduce_fusion.1
  116.4 0.2 fusion.14
  116.6 1.1 fusion
  117.7 0.6 copy.29
  118.3 1.1 reshape.199
  119.4 26.8 %all-gather.8.cloned.1.call-done = f32[1024,1024]{1,0:T(8,128)} async-done(((f32[256,1024]{1,0:T(8,128)}), f32[1024,1024]{1,0:T(8,128)}) %all-gather.8.cloned.1.call-update) | async-done | bytes 4194320 | tf_op jit(solution)/shard_map/all_gather | solution.py:127
  146.2 5.4 %copy.32 = f32[1024,1024]{1,0:T(8,128)} copy(f32[1024,1024]{0,1:T(8,128)} %bitcast.100) | data formatting | bytes 8388608 | tf_op jit(solution)/shard_map/dot_general | solution.py:125
  151.7 5.6 %convolution_bitcast_fusion = f32[32,8,8,128]{3,2,0,1:T(8,128)S(1)} fusion(f32[32,8,1024,1]{2,1,0,3:T(8,128)S(1)} %copy-done.3, f32[8,128,1024,1]{2,1,3,0:T(8,128)} %bitcast.91), kind=kOutput, calls=%fused_computation.14 | convolution fusion | flops 3221225472 | bytes 6291456 | tf_op jit(solution)/shard_map/dot_general | solution.py:125
  157.3 1.1 convolution_bitcast_fusion.1
  158.5 2.5 gather_fusion.4
  161.0 4.4 %select_select_fusion = f32[384,8,128]{2,1,0:T(8,128)} fusion(f32[384,8,128]{2,1,0:T(8,128)} %gather_fusion.4, pred[384]{0:T(512)(128)(4,1)S(1)} %compare_and_fusion.1, pred[384]{0:T(512)(128)(4,1)S(1)} %fusion.14), kind=kLoop, calls=%fused_computation.9 | loop fusion | flops 786432 | bytes 3146496 | tf_op jit(solution)/shard_map/jit(_where)/select_n | solution.py:42
  165.4 5.5 %all-to-all-start.2 = ((f32[384,8,128]{2,1,0:T(8,128)}), f32[384,8,128]{2,1,0:T(8,128)S(1)}, u32[]{:S(2)}, u32[]{:S(2)}) async-start(f32[384,8,128]{2,1,0:T(8,128)} %select_select_fusion), calls=%async_computation.2 | async-start | bytes 3145728 | tf_op jit(solution)/shard_map/all_to_all | solution.py:132
  171.0 37.4 %all-to-all-done.2 = f32[384,8,128]{2,1,0:T(8,128)S(1)} async-done(((f32[384,8,128]{2,1,0:T(8,128)}), f32[384,8,128]{2,1,0:T(8,128)S(1)}, u32[]{:S(2)}, u32[]{:S(2)}) %all-to-all-start.2) | async-done | bytes 1572896 | tf_op jit(solution)/shard_map/all_to_all | solution.py:132
  208.4 2.0 gather_fusion.5
  210.4 1.6 broadcast_select_fusion
  211.9 0.2 copy.51
  212.1 1.4 all_to_all.26
  213.6 2.4 copy.35
  216.0 4.6 %all-to-all-start.3 = ((f32[256,4,256]{2,0,1:T(8,128)}), f32[256,4,256]{2,0,1:T(8,128)}, u32[]{:S(2)}, u32[]{:S(2)}) async-start(f32[256,4,256]{2,0,1:T(8,128)} %copy.35), calls=%async_computation.3 | async-start | bytes 2097152 | tf_op jit(solution)/shard_map/all_to_all | solution.py:140
  221.3 7.2 %fusion.6 = f32[256,1024]{1,0:T(8,128)} fusion(f32[1024,1024]{1,0:T(8,128)} %all-gather.4.cloned.1.call-done, f32[256,1024]{1,0:T(8,128)} %get-tuple-element.10, f32[1024]{0:T(1024)S(1)} %bitcast.103), kind=kOutput, calls=%fused_computation.30 | convolution fusion | flops 3221487616 | bytes 6295552 | tf_op jit(solution)/shard_map/dot_general | solution.py:111
  228.5 6.4 %all-to-all-done.3 = f32[256,4,256]{2,0,1:T(8,128)} async-done(((f32[256,4,256]{2,0,1:T(8,128)}), f32[256,4,256]{2,0,1:T(8,128)}, u32[]{:S(2)}, u32[]{:S(2)}) %all-to-all-start.3) | async-done | bytes 1048608 | tf_op jit(solution)/shard_map/all_to_all | solution.py:140
  234.9 2.5 copy.39
  237.4 7.8 %select_reduce_fusion = (f32[256]{0:T(256)S(1)}, f32[256,1024]{1,0:T(8,128)}) fusion(s32[256]{0:T(256)S(1)} %iota_add_fusion, f32[1024]{0:T(1024)S(1)} %fusion.21, f32[256]{0:T(256)S(1)} %compare_convert_fusion, f32[1024,256]{0,1:T(8,128)} %copy.39, f32[32,8,8,128]{3,2,1,0:T(8,128)S(1)} %bitcast.93, f32[256,1024]{1,0:T(8,128)} %fusion.6, ...), kind=kOutput, calls=%fused_computation.27 | convolution fusion | flops 3224108800 | bytes 9448448 | tf_op jit(solution)/shard_map/dot_general | solution.py:117
  245.2 0.2 fusion.17
  245.4 37.6 %psum.7 = f32[240]{0:T(256)S(1)} all-reduce(f32[240]{0:T(256)S(1)} %bitcast.111), channel_id=1, replica_groups=mesh['chan'=8,'row'=4] {'chan','row'}, use_global_device_ids=true, to_apply=%region_7.10 | all-reduce | flops 240 | bytes 1920 | tf_op jit(solution)/shard_map/psum | solution.py:152
  283.0 0.6 broadcast_multiply_fusion
  (39 shorter events, 0.4 us)
Async XLA Ops:
  7.2 102.4 %copy-start = (f32[1,8,128,128]{3,2,1,0:T(8,128)S(1)}, f32[1,8,128,128]{3,2,1,0:T(8,128)}, u32[]{:S(2)}) copy-start(f32[1,8,128,128]{3,2,1,0:T(8,128)} %param.19) | copy-start | bytes 1572868
  14.1 2.5 copy-start.2
  65.3 3.8 %copy-start.5 = (s32[1,1,256]{2,1,0:T(1,128)S(1)}, s32[1,1,256]{2,1,0:T(1,128)}, u32[]{:S(2)}) copy-start(s32[1,1,256]{2,1,0:T(1,128)} %param.23) | copy-start | bytes 3076
  65.3 40.4 %all-to-all-start.1 = ((f32[384,8,128]{2,1,0:T(8,128)}), f32[384,8,128]{2,1,0:T(8,128)S(1)}, u32[]{:S(2)}, u32[]{:S(2)}) async-start(f32[384,8,128]{2,1,0:T(8,128)} %get-tuple-element.12), calls=%async_computation.1 | async-start | bytes 3145728 | tf_op jit(solution)/shard_map/all_to_all | solution.py:94
  69.0 77.2 %all-gather.8.cloned.1.call-start = ((), (), s32[]{:S(2)}) async-start(), calls=%async_computation.6 | async-start | bytes 5242880 | tf_op jit(solution)/shard_map/all_gather | solution.py:127
  111.2 1.5 copy-start.1
  112.5 108.7 %all-gather.4.cloned.1.call-start = ((), (), s32[]{:S(2)}) async-start(), calls=%async_computation.4 | async-start | bytes 5242880 | tf_op jit(solution)/shard_map/all_gather | solution.py:113
  115.5 1.1 copy-start.6
  115.5 121.9 %all-gather.6.cloned.1.call-start = ((), (), s32[]{:S(2)}) async-start(), calls=%async_computation.5 | async-start | bytes 5242880 | tf_op jit(solution)/shard_map/all_gather | solution.py:119
  146.2 5.4 %copy-start.3 = (f32[32,8,1024,1]{2,1,0,3:T(8,128)S(1)}, f32[32,8,1024,1]{2,1,0,3:T(8,128)}, u32[]{:S(2)}) copy-start(f32[32,8,1024,1]{2,1,0,3:T(8,128)} %reshape.199) | copy-start | bytes 3145732
  165.4 43.0 %all-to-all-start.2 = ((f32[384,8,128]{2,1,0:T(8,128)}), f32[384,8,128]{2,1,0:T(8,128)S(1)}, u32[]{:S(2)}, u32[]{:S(2)}) async-start(f32[384,8,128]{2,1,0:T(8,128)} %select_select_fusion), calls=%async_computation.2 | async-start | bytes 3145728 | tf_op jit(solution)/shard_map/all_to_all | solution.py:132
  216.0 5.3 %copy-start.4 = (f32[1,1024]{1,0:T(1,128)S(1)}, f32[1,1024]{1,0:T(1,128)}, u32[]{:S(2)}) copy-start(f32[1,1024]{1,0:T(1,128)} %param.17) | copy-start | bytes 12292
  216.0 18.9 %all-to-all-start.3 = ((f32[256,4,256]{2,0,1:T(8,128)}), f32[256,4,256]{2,0,1:T(8,128)}, u32[]{:S(2)}, u32[]{:S(2)}) async-start(f32[256,4,256]{2,0,1:T(8,128)} %copy.35), calls=%async_computation.3 | async-start | bytes 2097152 | tf_op jit(solution)/shard_map/all_to_all | solution.py:140
  237.4 7.8 %copy-start.7 = (s32[1,256]{1,0:T(1,128)S(1)}, s32[1,256]{1,0:T(1,128)}, u32[]{:S(2)}) copy-start(s32[1,256]{1,0:T(1,128)} %param.21) | copy-start | bytes 3076
Sparse Core Ops, SparseCore 0:
  112.6 33.5 all-gather.7
  147.8 34.4 all-gather.3
  183.8 34.4 all-gather.5
where the time goes:
time: 291 us; the launch traced here: 290 us
  waiting for transfers between devices  104 us (36%)
  blocking collectives  81.8 us (28%)
  local copies, waits for them, and re-layouts  30.6 us (11%)
  matrix products  24 us (8%)
  other arithmetic  20 us (7%)
  between operations  15.3 us (5%)
  starting transfers between devices  14.1 us (5%)
    all_to_all x1, blocking collectives, per_device(): lax.all_to_all(pack_slots(cut_tiles(eta_rows), send_slot, slot_total), 'c...  44.2 us
    psum x1, blocking collectives, per_device(): gathered_sum = lax.psum(partial_value, ('chan', 'row'))  37.6 us
    all_to_all x1, waiting for transfers between devices, per_device(): lax.all_to_all(pack_slots(back_tiles, recv_slot, slot_total), 'chan', spl...  37.4 us
    all_to_all x1, waiting for transfers between devices, per_device(): lax.all_to_all(pack_slots(cut_tiles(ham_rows), send_slot, slot_total), 'c...  33.2 us
    all_gather x1, waiting for transfers between devices, per_device(): lax.all_gather(ph_ham, 'row', axis=0, tiled=True)  26.8 us
    select_n x2, other arithmetic, pack_slots(): return jnp.where(filled.reshape(mask_shape), picked, jnp.zeros_like(picked))  8.93 us
    dot_general x1, matrix products, per_device(): jnp.dot(ham_part, lax.all_gather(eta_rows, 'row', axis=0, tiled=True), pr...  7.75 us
    gather x3, local copies, waits for them, and re-layouts, pack_slots(): picked = jnp.take(tile_set, source, axis=0)  7.55 us
  transfers between devices with their start and end apart: 6, of which 4 were waited for; matrix products, arithmetic and copies ran while one was open for 15% of the time, Pallas kernels for 0%

commit v1 on v0

v1 whole, which is shorter than its diff:
```python
import functools
import math

import jax
import jax.numpy as jnp
from jax import lax
from jax.experimental import pallas as pl
from jax.experimental.pallas import tpu as pltpu
from jax.sharding import PartitionSpec as P

TW = 128
TR = 8
NORB = 240
OPAD = 256
MESH = pl.DeviceIdType.MESH
F32 = jnp.float32
BF16 = jnp.bfloat16
ROW_DIMS = (((1,), (1,)), ((), ()))
COL_DIMS = (((1,), (0,)), ((), ()))


def group_rank(labels):
    length = labels.shape[-1]
    position = jnp.arange(length, dtype=jnp.int32)
    same_label = labels[:, :, None] == labels[:, None, :]
    before = position[None, :] < position[:, None]
    return jnp.sum((same_label & before).astype(jnp.int32), axis=-1)


def split(value):
    high = value.astype(BF16)
    return high, (value - high.astype(F32)).astype(BF16)


def dot3(left, right, dims=COL_DIMS):
    mul = functools.partial(lax.dot_general, dimension_numbers=dims, preferred_element_type=F32)
    return mul(left[0], right[0]) + (mul(left[0], right[1]) + mul(left[1], right[0]))


def kernel(
    n,
    cap,
    eta_ref,
    ham_ref,
    size_ref,
    pp_ref,
    ph_ref,
    coup_ref,
    weight_ref,
    orbit_ref,
    pack_ref,
    take_ref,
    back_pack_ref,
    back_take_ref,
    comm_ref,
    onebody_ref,
    ham_tiles,
    eta_tiles,
    ham_send,
    eta_send,
    ham_recv,
    eta_recv,
    full_ham,
    full_ph,
    mixed,
    left_hi,
    left_lo,
    lad_hi,
    lad_lo,
    total,
    back_send,
    back_recv,
    turned_send,
    turned_recv,
    row_sums,
    chan_sums,
    a2a_send,
    a2a_recv,
    gather_send,
    gather_recv,
    turn_send,
    turn_recv,
    rsum_send,
    rsum_recv,
    csum_send,
    csum_recv,
):
    me = lax.axis_index("chan")
    row = lax.axis_index("row")
    rows, cols = eta_ref.shape
    rgroups = cols // rows
    bands = cols // TW
    groups = rows // TR
    near = row + 1 - 2 * lax.rem(row, 2)
    far = lax.rem(row + 2, rgroups)
    diagonal_peer = lax.rem(near + 2, rgroups)
    half = n // 2

    def chan_peer(step):
        away = step // 2
        sign = 2 * lax.rem(step, 2) - 1
        return lax.rem(me + half + sign * away + n, n)

    barrier = pltpu.get_barrier_semaphore()

    @pl.loop(1, n)
    def _(step):
        pl.semaphore_signal(
            barrier, inc=1, device_id=(chan_peer(step), row), device_id_type=MESH
        )

    for other in range(1, rgroups):
        pl.semaphore_signal(
            barrier,
            inc=1,
            device_id=(me, lax.rem(row + other, rgroups)),
            device_id_type=MESH,
        )

    size = size_ref[0]
    row_ids = row * rows + lax.broadcasted_iota(jnp.int32, (rows, TW), 0)
    lane_ids = lax.broadcasted_iota(jnp.int32, (rows, TW), 1)

    def mask_of(band):
        return (row_ids < size) & (lane_ids + band * TW < size)

    for band in range(bands):
        lanes = slice(band * TW, (band + 1) * TW)
        value = jnp.where(mask_of(band), ham_ref[:, lanes], 0.0)
        full_ham[row, :, lanes] = value
        ham_tiles[band * groups : (band + 1) * groups] = value.reshape(groups, TR, TW)

    pl.semaphore_wait(barrier, n - 1 + rgroups - 1)

    def gather_copy(buf, phase, kind, slot, target):
        return pltpu.make_async_remote_copy(
            src_ref=buf.at[slot],
            dst_ref=buf.at[slot],
            send_sem=gather_send.at[phase, kind],
            recv_sem=gather_recv.at[phase, kind],
            device_id=(me, target),
            device_id_type=MESH,
        )

    def gather_start(buf, phase):
        gather_copy(buf, phase, 0, row, far).start()
        gather_copy(buf, phase, 1, row, near).start()

    def gather_forward(buf, phase):
        gather_copy(buf, phase, 0, far, far).wait_recv()
        gather_copy(buf, phase, 2, far, near).start()

    def gather_finish(buf, phase):
        gather_copy(buf, phase, 1, near, near).wait_recv()
        gather_copy(buf, phase, 2, diagonal_peer, near).wait_recv()

    def gather_drain(buf, phase):
        gather_copy(buf, phase, 0, row, far).wait_send()
        gather_copy(buf, phase, 1, row, near).wait_send()
        gather_copy(buf, phase, 2, far, near).wait_send()

    unit = next(u for u in (16, 12, 8, 6, 4, 3, 2, 1) if cap % u == 0)

    def pack_one(tiles, out, table, peer, base):
        @pl.loop(0, cap // unit)
        def _(part):
            for inner in range(unit):
                place = part * unit + inner
                out[base + place] = tiles[table[peer * cap + place]]

    def send_copy(send, recv, phase, peer, source):
        return pltpu.make_async_remote_copy(
            src_ref=send.at[pl.ds(peer * cap, cap)],
            dst_ref=recv.at[pl.ds(source * cap, cap)],
            send_sem=a2a_send.at[phase, peer],
            recv_sem=a2a_recv.at[phase, source],
            device_id=(peer, row),
            device_id_type=MESH,
        )

    def pack_send(tiles, send, recv, table, phase):
        @pl.loop(1, n)
        def _(step):
            peer = chan_peer(step)
            pack_one(tiles, send, table, peer, peer * cap)
            send_copy(send, recv, phase, peer, me).start()

        pack_one(tiles, recv, table, me, me * cap)

    def wait_sent(send, recv, phase):
        @pl.loop(1, n)
        def _(step):
            send_copy(send, recv, phase, chan_peer(step), me).wait_send()

    def wait_arrived(send, recv, phase):
        @pl.loop(1, n)
        def _(step):
            peer = chan_peer(step)
            send_copy(send, recv, phase, peer, peer).wait_recv()

    pack_send(ham_tiles, ham_send, ham_recv, pack_ref, 0)
    gather_start(full_ham, 0)

    for band in range(bands):
        lanes = slice(band * TW, (band + 1) * TW)
        value = jnp.where(mask_of(band), eta_ref[:, lanes], 0.0)
        eta_tiles[band * groups : (band + 1) * groups] = value.reshape(groups, TR, TW)
        high, low = split(value * pp_ref[:, lanes])
        lad_hi[:, lanes] = high
        lad_lo[:, lanes] = low

    wait_sent(ham_send, ham_recv, 0)
    pack_send(eta_tiles, eta_send, eta_recv, pack_ref, 1)

    def unpack(recv):
        @pl.loop(0, groups * bands // 16)
        def _(part):
            for inner in range(16):
                place = part * 16 + inner
                mixed[place] = recv[take_ref[place]]

    def mixed_band(band):
        tiles = mixed[band * groups : (band + 1) * groups].reshape(rows, TW)
        return dot3(split(tiles), split(coup_ref[band]))

    wait_arrived(ham_send, ham_recv, 0)
    unpack(ham_recv)
    for band in range(bands):
        full_ph[row, :, band * TW : (band + 1) * TW] = mixed_band(band)
    gather_start(full_ph, 1)
    gather_forward(full_ham, 0)
    gather_forward(full_ph, 1)

    wait_arrived(eta_send, eta_recv, 1)
    unpack(eta_recv)
    for band in range(bands):
        lanes = slice(band * TW, (band + 1) * TW)
        high, low = split(mixed_band(band) * ph_ref[:, lanes])
        left_hi[:, lanes] = high
        left_lo[:, lanes] = low
    gather_finish(full_ph, 1)

    def multiply(high_ref, low_ref, full):
        @pl.loop(0, cols // 256)
        def _(part):
            lanes = pl.ds(pl.multiple_of(part * 256, 256), 256)
            result = None
            for block in range(rgroups):
                depth = slice(block * rows, (block + 1) * rows)
                term = dot3(
                    (high_ref[:, depth], low_ref[:, depth]), split(full[block, :, lanes])
                )
                result = term if result is None else result + term
            total[:, lanes] = result

    multiply(left_hi, left_lo, full_ph)
    for band in range(bands):
        lanes = slice(band * TW, (band + 1) * TW)
        value = dot3(split(total[:, lanes]), split(coup_ref[band]), ROW_DIMS)
        mixed[band * groups : (band + 1) * groups] = value.reshape(groups, TR, TW)
    pack_send(mixed, back_send, back_recv, back_pack_ref, 2)

    gather_finish(full_ham, 0)
    multiply(lad_hi, lad_lo, full_ham)
    wait_sent(eta_send, eta_recv, 1)
    gather_drain(full_ham, 0)
    gather_drain(full_ph, 1)

    wait_arrived(back_send, back_recv, 2)

    @pl.loop(0, groups)
    def _(group):
        spot = pl.ds(pl.multiple_of(group * TR, TR), TR)
        for band in range(bands):
            lanes = slice(band * TW, (band + 1) * TW)
            total[spot, lanes] += back_recv[back_take_ref[group * bands + band]]

    def turn_copy(target, source):
        return pltpu.make_async_remote_copy(
            src_ref=turned_send.at[target],
            dst_ref=turned_recv.at[source],
            send_sem=turn_send.at[target],
            recv_sem=turn_recv.at[source],
            device_id=(me, target),
            device_id_type=MESH,
        )

    def block_of(target):
        return total[:, pl.ds(pl.multiple_of(target * rows, rows), rows)]

    for target in (far, diagonal_peer, near):
        turned_send[target] = block_of(target).T
        turn_copy(target, row).start()

    own = block_of(row)
    turned_recv[row] = own.T
    eye_rows = lax.broadcasted_iota(jnp.int32, (rows, rows), 0)
    eye_cols = lax.broadcasted_iota(jnp.int32, (rows, rows), 1)
    diagonal = jnp.sum(jnp.where(eye_rows == eye_cols, own, 0.0), axis=0, keepdims=True)
    alive = row * rows + lax.broadcasted_iota(jnp.int32, (1, rows), 1) < size
    terms = jnp.where(alive, (diagonal + diagonal) * weight_ref[0], 0.0)
    orbit_ids = lax.broadcasted_iota(jnp.int32, (OPAD, rows), 0)
    table = (orbit_ids == orbit_ref[...]).astype(F32)
    row_sums[row] = lax.dot_general(
        jnp.broadcast_to(terms, (TR, rows)),
        table,
        ROW_DIMS,
        precision=lax.Precision.HIGHEST,
        preferred_element_type=F32,
    )

    def rsum_copy(target, source):
        return pltpu.make_async_remote_copy(
            src_ref=row_sums.at[row],
            dst_ref=row_sums.at[source],
            send_sem=rsum_send.at[target],
            recv_sem=rsum_recv.at[source],
            device_id=(me, target),
            device_id_type=MESH,
        )

    for target in (far, diagonal_peer, near):
        rsum_copy(target, row).start()
    for target in (far, diagonal_peer, near):
        rsum_copy(target, target).wait_recv()
    partial_value = row_sums[0]
    for block in range(1, rgroups):
        partial_value = partial_value + row_sums[block]
    chan_sums[me] = partial_value

    def csum_copy(target, source):
        return pltpu.make_async_remote_copy(
            src_ref=chan_sums.at[me],
            dst_ref=chan_sums.at[source],
            send_sem=csum_send.at[target],
            recv_sem=csum_recv.at[source],
            device_id=(target, row),
            device_id_type=MESH,
        )

    @pl.loop(1, n)
    def _(step):
        csum_copy(chan_peer(step), me).start()

    for target in (near, far, diagonal_peer):
        turn_copy(target, target).wait_recv()
    for block in range(rgroups):
        for part in range(rows // TW):
            band = block * (rows // TW) + part
            lanes = slice(band * TW, (band + 1) * TW)
            value = total[:, lanes] + turned_recv[block, :, part * TW : (part + 1) * TW]
            comm_ref[:, lanes] = jnp.where(mask_of(band), value, 0.0)

    @pl.loop(1, n)
    def _(step):
        peer = chan_peer(step)
        csum_copy(peer, peer).wait_recv()

    onebody_ref[...] = lax.fori_loop(
        0, n, lambda i, acc: acc + chan_sums[i], jnp.zeros((TR, OPAD), F32)
    ) * math.sqrt(NORB / (n * cols))

    wait_sent(back_send, back_recv, 2)
    for target in (far, diagonal_peer, near):
        turn_copy(target, row).wait_send()
        rsum_copy(target, row).wait_send()

    @pl.loop(1, n)
    def _(step):
        csum_copy(chan_peer(step), me).wait_send()


def per_device(
    eta_pp,
    ham_pp,
    block_size,
    pp_occupancy,
    ph_occupancy,
    coupling,
    channel_weight,
    orbit_of,
    tile_target,
    tile_source,
):
    rows, cols = eta_pp.shape[1:]
    n = lax.axis_size("chan")
    rgroups = lax.axis_size("row")
    bands, groups = cols // TW, rows // TR
    count = bands * groups
    cap = max(2, 3 * count // (2 * n))
    slots = cap * n

    labels = jnp.stack([tile_target[0, 0], tile_source[0, 0]])
    slot_of = labels * cap + group_rank(labels)
    position = jnp.arange(count, dtype=jnp.int32)
    by_band = position % bands * groups + position // bands
    matches = slot_of[:, None, :] == jnp.arange(slots, dtype=jnp.int32)[None, :, None]
    pack = jnp.sum(jnp.where(matches, by_band, 0), axis=-1)
    take = slot_of[1].reshape(groups, bands).T.reshape(count)

    vmem = pl.BlockSpec(memory_space=pltpu.VMEM)
    smem = pl.BlockSpec(memory_space=pltpu.SMEM)
    dma = pltpu.SemaphoreType.DMA
    tile_buf = pltpu.VMEM((count, TR, TW), F32)
    slot_buf = pltpu.VMEM((slots, TR, TW), F32)
    full_buf = pltpu.VMEM((rgroups, rows, cols), F32)
    half_buf = pltpu.VMEM((rows, cols), BF16)
    comm, onebody = pl.pallas_call(
        functools.partial(kernel, n, cap),
        out_shape=(
            jax.ShapeDtypeStruct((rows, cols), F32),
            jax.ShapeDtypeStruct((TR, OPAD), F32),
        ),
        in_specs=[vmem, vmem, smem, vmem, vmem, vmem, smem, vmem, smem, smem, smem, smem],
        out_specs=(vmem, vmem),
        scratch_shapes=[
            tile_buf,
            tile_buf,
            slot_buf,
            slot_buf,
            slot_buf,
            slot_buf,
            full_buf,
            full_buf,
            tile_buf,
            half_buf,
            half_buf,
            half_buf,
            half_buf,
            pltpu.VMEM((rows, cols), F32),
            slot_buf,
            slot_buf,
            pltpu.VMEM((rgroups, rows, rows), F32),
            pltpu.VMEM((rgroups, rows, rows), F32),
            pltpu.VMEM((rgroups, TR, OPAD), F32),
            pltpu.VMEM((n, TR, OPAD), F32),
            dma((3, n)),
            dma((3, n)),
            dma((2, 3)),
            dma((2, 3)),
            dma((rgroups,)),
            dma((rgroups,)),
            dma((rgroups,)),
            dma((rgroups,)),
            dma((n,)),
            dma((n,)),
        ],
        compiler_params=pltpu.CompilerParams(
            collective_id=0, has_side_effects=True, vmem_limit_bytes=48 * 1024 * 1024
        ),
    )(
        eta_pp[0],
        ham_pp[0],
        block_size,
        pp_occupancy,
        ph_occupancy,
        coupling[0],
        channel_weight,
        orbit_of,
        pack[0],
        take,
        pack[1],
        slot_of[0],
    )
    return comm[None], onebody[0, :NORB]


def solution(mesh):
    return jax.shard_map(
        per_device,
        mesh=mesh,
        in_specs=(
            P("chan", "row", None),
            P("chan", "row", None),
            P("chan"),
            P("chan", None),
            P("chan", None),
            P("chan", None, None, None),
            P("chan"),
            P("chan", "row"),
            P("chan", "row", None),
            P("chan", "row", None),
        ),
        out_specs=(P("chan", "row", None), P()),
        check_vma=False,
    )
```

time: 291 us -> 144 us (0.49)
  Pallas kernels: 0 us -> 135 us
  waiting for transfers between devices: 104 us -> 0 us
  blocking collectives: 81.8 us -> 0 us
  local copies, waits for them, and re-layouts: 30.6 us -> 6.58 us
  matrix products: 24 us -> 0 us
  other arithmetic: 20 us -> 0.49 us
  starting transfers between devices: 14.1 us -> 0 us
  between operations: 15.3 us -> 1.98 us
    pallas_call x0 -> x1, Pallas kernels: none -> 135 us  [per_device(): pl.pallas_call(functools.partial(kernel, n, cap), out_shape=(jax.ShapeDty...]
    all_to_all x3 -> x0, waiting for transfers between devices: 77 us -> none  [the longest x1 37.4 us: per_device(): lax.all_to_all(pack_slots(back_tiles, recv_slot, slot_total), 'chan', spl...]
    all_to_all x1 -> x0, blocking collectives: 44.2 us -> none  [per_device(): lax.all_to_all(pack_slots(cut_tiles(eta_rows), send_slot, slot_total), 'c...]
    psum x1 -> x0, blocking collectives: 37.6 us -> none  [per_device(): gathered_sum = lax.psum(partial_value, ('chan', 'row'))]
    all_gather x3 -> x0, waiting for transfers between devices: 26.8 us -> none  [the longest x1 26.8 us: per_device(): lax.all_gather(ph_ham, 'row', axis=0, tiled=True)]
    dot_general x7 -> x0, matrix products: 24 us -> none  [the longest x1 7.75 us: per_device(): jnp.dot(ham_part, lax.all_gather(eta_rows, 'row', axis=0, tiled=True), pr...]
    gather x6 -> x0, local copies, waits for them, and re-layouts: 14.7 us -> none  [the longest x3 7.55 us: pack_slots(): picked = jnp.take(tile_set, source, axis=0)]
    all_to_all x3 -> x0, starting transfers between devices: 13.8 us -> none  [the longest x1 5.52 us: per_device(): lax.all_to_all(pack_slots(back_tiles, recv_slot, slot_total), 'chan', spl...]
  transfers between devices with their start and end apart: 6 -> 0, of which waited for: 4 -> 0; matrix products, arithmetic and copies ran while one was open for 15% -> 0% of each run, Pallas kernels for 0% -> 0%
where the time goes in v1:
time: 144 us
  Pallas kernels  135 us (94%)
  local copies, waits for them, and re-layouts  6.58 us (5%)
  between operations  1.98 us (1%)
    pallas_call x1, Pallas kernels, per_device(): pl.pallas_call(functools.partial(kernel, n, cap), out_shape=(jax.ShapeDty...  135 us
    unnamed x17, local copies, waits for them, and re-layouts  5.75 us

profile of v1, /device:TPU:0, one launch (start us, length us, event | category | flops | bytes accessed | tf_op | source)
XLA Modules:
  0.0 144.0 jit_solution(7555435389631173046)
XLA Ops:
  1.9 0.0 copy-start.7
  1.9 0.0 copy-start.6
  2.0 0.6 copy-done.7
  2.6 0.0 copy-done.6
  2.7 0.2 convert_reduce_fusion
  2.9 0.2 select_reduce_fusion
  3.2 0.1 reshape_squeeze.3
  3.2 0.0 copy-start.4
  3.2 0.1 copy.13
  3.3 0.0 copy-start.3
  3.3 0.0 copy-start.5
  3.3 0.1 reshape.39.take_ref
  3.4 0.5 copy-done.4
  3.9 0.1 copy-done.3
  4.0 0.0 copy-done.5
  4.0 0.0 copy-start
  4.0 1.2 copy-done
  5.2 0.0 copy-start.1
  5.2 1.2 copy-done.1
  6.5 0.0 copy-start.2
  6.5 1.0 copy-done.2
  7.5 134.9 %shard_map.113 = (f32[256,1024]{1,0:T(8,128)S(1)}, f32[8,256]{1,0:T(8,128)S(1)}) custom-call(f32[256,1024]{1,0:T(8,128)S(1)} %bitcast.9, f32[256,1024]{1,0:T(8,128)S(1)} %bitcast.10, s32[1]{0:T(128)S(6)} %copy.15.size_ref, f32[1,1024]{1,0:T(1,128)S(1)} %copy-done.3, f32[1,1024]{1,0:T(1,128)S(1)} %copy-done.4, f32[8,128,128]{2,1,0:T(8,128)S(1)} %bitcast.12, ...), custom_call_target="tpu_custom_call" | custom-call | tf_op jit(solution)/shard_map/pallas_call | solution.py:408
  142.5 0.6 slice.19
  143.0 1.0 copy.17
  (6 shorter events, 0.1 us)
Async XLA Ops:
  1.9 0.7 copy-start.7
  1.9 0.7 copy-start.6
  3.2 0.7 copy-start.4
  3.3 0.7 copy-start.3
  3.3 0.7 copy-start.5
  4.0 1.2 copy-start
  5.2 1.2 copy-start.1
  6.5 1.0 copy-start.2

commit v2 on v1

--- a/solution.py
+++ b/solution.py
@@ -40,12 +40,12 @@
 def kernel(
     n,
     cap,
-    eta_ref,
-    ham_ref,
+    eta_hbm,
+    ham_hbm,
     size_ref,
     pp_ref,
     ph_ref,
-    coup_ref,
+    coup_hbm,
     weight_ref,
     orbit_ref,
     pack_ref,
@@ -54,6 +54,12 @@
     back_take_ref,
     comm_ref,
     onebody_ref,
+    eta_ref,
+    ham_ref,
+    coup_ref,
+    squares,
+    ph_hi,
+    ph_lo,
     ham_tiles,
     eta_tiles,
     ham_send,
@@ -74,6 +80,7 @@
     turned_recv,
     row_sums,
     chan_sums,
+    load_sem,
     a2a_send,
     a2a_recv,
     gather_send,
@@ -101,6 +108,15 @@
         sign = 2 * lax.rem(step, 2) - 1
         return lax.rem(me + half + sign * away + n, n)
 
+    loads = [
+        pltpu.make_async_copy(source, target, load_sem.at[place])
+        for place, (source, target) in enumerate(
+            ((ham_hbm, ham_ref), (eta_hbm, eta_ref), (coup_hbm, coup_ref))
+        )
+    ]
+    for load in loads:
+        load.start()
+
     barrier = pltpu.get_barrier_semaphore()
 
     @pl.loop(1, n)
@@ -124,6 +140,7 @@
     def mask_of(band):
         return (row_ids < size) & (lane_ids + band * TW < size)
 
+    loads[0].wait()
     for band in range(bands):
         lanes = slice(band * TW, (band + 1) * TW)
         value = jnp.where(mask_of(band), ham_ref[:, lanes], 0.0)
@@ -201,6 +218,7 @@
     pack_send(ham_tiles, ham_send, ham_recv, pack_ref, 0)
     gather_start(full_ham, 0)
 
+    loads[1].wait()
     for band in range(bands):
         lanes = slice(band * TW, (band + 1) * TW)
         value = jnp.where(mask_of(band), eta_ref[:, lanes], 0.0)
@@ -219,49 +237,75 @@
                 place = part * 16 + inner
                 mixed[place] = recv[take_ref[place]]
 
-    def mixed_band(band):
-        tiles = mixed[band * groups : (band + 1) * groups].reshape(rows, TW)
-        return dot3(split(tiles), split(coup_ref[band]))
+    def band_tiles(band):
+        return mixed[band * groups : (band + 1) * groups].reshape(rows, TW)
+
+    loads[2].wait()
+    for band in range(bands):
+        square = split(coup_ref[band])
+        squares[band] = dot3(square, square, ROW_DIMS)
 
     wait_arrived(ham_send, ham_recv, 0)
     unpack(ham_recv)
     for band in range(bands):
-        full_ph[row, :, band * TW : (band + 1) * TW] = mixed_band(band)
+        total[:, band * TW : (band + 1) * TW] = dot3(
+            split(band_tiles(band)), split(squares[band])
+        )
+    for part in range(rows // TW):
+        band = row * (rows // TW) + part
+        factors = ph_ref[:, pl.ds(pl.multiple_of(band * TW, TW), TW)]
+        spot = slice(part * TW, (part + 1) * TW)
+        full_ph[row, spot] = dot3(split(coup_ref[band] * factors), split(total[spot]))
     gather_start(full_ph, 1)
     gather_forward(full_ham, 0)
     gather_forward(full_ph, 1)
+
+    gather_finish(full_ph, 1)
+    for block in range(rgroups):
+        high, low = split(full_ph[block])
+        ph_hi[block] = high
+        ph_lo[block] = low
 
     wait_arrived(eta_send, eta_recv, 1)
     unpack(eta_recv)
     for band in range(bands):
         lanes = slice(band * TW, (band + 1) * TW)
-        high, low = split(mixed_band(band) * ph_ref[:, lanes])
+        high, low = split(band_tiles(band))
         left_hi[:, lanes] = high
         left_lo[:, lanes] = low
-    gather_finish(full_ph, 1)
-
-    def multiply(high_ref, low_ref, full):
+
+    def multiply(high_ref, low_ref, right, write):
         @pl.loop(0, cols // 256)
         def _(part):
             lanes = pl.ds(pl.multiple_of(part * 256, 256), 256)
             result = None
             for block in range(rgroups):
                 depth = slice(block * rows, (block + 1) * rows)
-                term = dot3(
-                    (high_ref[:, depth], low_ref[:, depth]), split(full[block, :, lanes])
-                )
+                term = dot3((high_ref[:, depth], low_ref[:, depth]), right(block, lanes))
                 result = term if result is None else result + term
-            total[:, lanes] = result
-
-    multiply(left_hi, left_lo, full_ph)
-    for band in range(bands):
-        lanes = slice(band * TW, (band + 1) * TW)
-        value = dot3(split(total[:, lanes]), split(coup_ref[band]), ROW_DIMS)
-        mixed[band * groups : (band + 1) * groups] = value.reshape(groups, TR, TW)
+            write(part, lanes, result)
+
+    def write_tiles(part, lanes, result):
+        for inner in range(256 // TW):
+            value = result[:, inner * TW : (inner + 1) * TW].reshape(groups, TR, TW)
+            band = part * (256 // TW) + inner
+            mixed[pl.ds(band * groups, groups)] = value
+
+    def write_rows(part, lanes, result):
+        total[:, lanes] = result
+
+    multiply(
+        left_hi,
+        left_lo,
+        lambda block, lanes: (ph_hi[block, :, lanes], ph_lo[block, :, lanes]),
+        write_tiles,
+    )
     pack_send(mixed, back_send, back_recv, back_pack_ref, 2)
 
     gather_finish(full_ham, 0)
-    multiply(lad_hi, lad_lo, full_ham)
+    multiply(
+        lad_hi, lad_lo, lambda block, lanes: split(full_ham[block, :, lanes]), write_rows
+    )
     wait_sent(eta_send, eta_recv, 1)
     gather_drain(full_ham, 0)
     gather_drain(full_ph, 1)
@@ -356,9 +400,10 @@
         peer = chan_peer(step)
         csum_copy(peer, peer).wait_recv()
 
-    onebody_ref[...] = lax.fori_loop(
+    sums = lax.fori_loop(
         0, n, lambda i, acc: acc + chan_sums[i], jnp.zeros((TR, OPAD), F32)
-    ) * math.sqrt(NORB / (n * cols))
+    )
+    onebody_ref[...] = sums[:1, :NORB] * math.sqrt(NORB / (n * cols))
 
     wait_sent(back_send, back_recv, 2)
     for target in (far, diagonal_peer, near):
@@ -399,6 +444,7 @@
     take = slot_of[1].reshape(groups, bands).T.reshape(count)
 
     vmem = pl.BlockSpec(memory_space=pltpu.VMEM)
+    hbm = pl.BlockSpec(memory_space=pl.ANY)
     smem = pl.BlockSpec(memory_space=pltpu.SMEM)
     dma = pltpu.SemaphoreType.DMA
     tile_buf = pltpu.VMEM((count, TR, TW), F32)
@@ -409,11 +455,17 @@
         functools.partial(kernel, n, cap),
         out_shape=(
             jax.ShapeDtypeStruct((rows, cols), F32),
-            jax.ShapeDtypeStruct((TR, OPAD), F32),
+            jax.ShapeDtypeStruct((1, NORB), F32),
         ),
-        in_specs=[vmem, vmem, smem, vmem, vmem, vmem, smem, vmem, smem, smem, smem, smem],
+        in_specs=[hbm, hbm, smem, vmem, vmem, hbm, smem, vmem, smem, smem, smem, smem],
         out_specs=(vmem, vmem),
         scratch_shapes=[
+            pltpu.VMEM((rows, cols), F32),
+            pltpu.VMEM((rows, cols), F32),
+            pltpu.VMEM((bands, TW, TW), F32),
+            pltpu.VMEM((bands, TW, TW), F32),
+            pltpu.VMEM((rgroups, rows, cols), BF16),
+            pltpu.VMEM((rgroups, rows, cols), BF16),
             tile_buf,
             tile_buf,
             slot_buf,
@@ -434,6 +486,7 @@
             pltpu.VMEM((rgroups, rows, rows), F32),
             pltpu.VMEM((rgroups, TR, OPAD), F32),
             pltpu.VMEM((n, TR, OPAD), F32),
+            dma((3,)),
             dma((3, n)),
             dma((3, n)),
             dma((2, 3)),
@@ -446,7 +499,7 @@
             dma((n,)),
         ],
         compiler_params=pltpu.CompilerParams(
-            collective_id=0, has_side_effects=True, vmem_limit_bytes=48 * 1024 * 1024
+            collective_id=0, has_side_effects=True, vmem_limit_bytes=56 * 1024 * 1024
         ),
     )(
         eta_pp[0],
@@ -462,7 +515,7 @@
         pack[1],
         slot_of[0],
     )
-    return comm[None], onebody[0, :NORB]
+    return comm[None], onebody.reshape(NORB)
 
 
 def solution(mesh):

time: 144 us -> 144 us (level)
    unnamed x17 -> x8, local copies, waits for them, and re-layouts: 5.75 us -> 3.54 us
where the time goes in v2:
time: 144 us; the launch traced here: 143 us
  Pallas kernels  135 us (94%)
  local copies, waits for them, and re-layouts  5.55 us (4%)
  between operations  1.97 us (1%)
    pallas_call x1, Pallas kernels, per_device(): pl.pallas_call(functools.partial(kernel, n, cap), out_shape=(jax.ShapeDty...  135 us
    unnamed x8, local copies, waits for them, and re-layouts  3.54 us

profile of v2, /device:TPU:0, one launch (start us, length us, event | category | flops | bytes accessed | tf_op | source)
XLA Modules:
  0.0 143.5 jit_solution(7947639170206830298)
XLA Ops:
  1.9 0.0 copy-start.1
  1.9 0.0 copy-start
  2.0 0.6 copy-done.1
  2.6 0.0 copy-done
  2.7 0.2 convert_reduce_fusion
  2.9 0.2 select_reduce_fusion
  3.1 0.6 fusion.4
  3.7 0.6 slice_reduce_fusion
  4.3 0.1 reshape_squeeze.3
  4.4 0.1 copy.13
  4.4 0.7 reshape.42.take_ref
  5.1 135.5 %shard_map.113 = (f32[256,1024]{1,0:T(8,128)}, f32[1,240]{1,0:T(1,128)}) custom-call(f32[256,1024]{1,0:T(8,128)} %bitcast.9, f32[256,1024]{1,0:T(8,128)} %bitcast.10, s32[1]{0:T(128)S(6)} %copy.16.size_ref, f32[1,1024]{1,0:T(1,128)} %pp_ref.1, f32[1,1024]{1,0:T(1,128)} %ph_ref.1, f32[8,128,128]{2,1,0:T(8,128)} %bitcast.12, f32[1]{0:T(128)S(6)} %copy.17.weight_ref, ...), custom_call_target="tpu_custom_call" | custom-call | tf_op jit(solution)/shard_map/pallas_call | solution.py:454
  140.6 0.0 copy-start.2
  140.6 2.3 %copy.18 = f32[1,256,1024]{2,1,0:T(8,128)} copy(f32[1,256,1024]{2,1,0:T(8,128)} %bitcast.11) | data formatting | bytes 2097152
  142.9 0.0 copy-done.2
  142.9 0.6 copy.19
  (4 shorter events, 0.1 us)
Async XLA Ops:
  1.9 0.7 copy-start.1
  1.9 0.7 copy-start
  140.6 2.3 %copy-start.2 = (f32[1,240]{1,0:T(1,128)S(1)}, f32[1,240]{1,0:T(1,128)}, u32[]{:S(2)}) copy-start(f32[1,240]{1,0:T(1,128)} %get-tuple-element.5) | copy-start | bytes 2884

commit v3 on v2

--- a/solution.py
+++ b/solution.py
@@ -149,32 +149,41 @@
 
     pl.semaphore_wait(barrier, n - 1 + rgroups - 1)
 
-    def gather_copy(buf, phase, kind, slot, target):
+    chunks = 4
+    chunk_rows = rows // chunks
+
+    def gather_copy(buf, phase, kind, slot, target, chunk):
+        place = buf.at[slot, pl.ds(chunk * chunk_rows, chunk_rows)]
         return pltpu.make_async_remote_copy(
-            src_ref=buf.at[slot],
-            dst_ref=buf.at[slot],
-            send_sem=gather_send.at[phase, kind],
-            recv_sem=gather_recv.at[phase, kind],
+            src_ref=place,
+            dst_ref=place,
+            send_sem=gather_send.at[phase, kind, chunk],
+            recv_sem=gather_recv.at[phase, kind, chunk],
             device_id=(me, target),
             device_id_type=MESH,
         )
 
     def gather_start(buf, phase):
-        gather_copy(buf, phase, 0, row, far).start()
-        gather_copy(buf, phase, 1, row, near).start()
+        for chunk in range(chunks):
+            gather_copy(buf, phase, 0, row, far, chunk).start()
+        for chunk in range(chunks):
+            gather_copy(buf, phase, 1, row, near, chunk).start()
 
     def gather_forward(buf, phase):
-        gather_copy(buf, phase, 0, far, far).wait_recv()
-        gather_copy(buf, phase, 2, far, near).start()
+        for chunk in range(chunks):
+            gather_copy(buf, phase, 0, far, far, chunk).wait_recv()
+            gather_copy(buf, phase, 2, far, near, chunk).start()
 
     def gather_finish(buf, phase):
-        gather_copy(buf, phase, 1, near, near).wait_recv()
-        gather_copy(buf, phase, 2, diagonal_peer, near).wait_recv()
+        for chunk in range(chunks):
+            gather_copy(buf, phase, 1, near, near, chunk).wait_recv()
+            gather_copy(buf, phase, 2, diagonal_peer, near, chunk).wait_recv()
 
     def gather_drain(buf, phase):
-        gather_copy(buf, phase, 0, row, far).wait_send()
-        gather_copy(buf, phase, 1, row, near).wait_send()
-        gather_copy(buf, phase, 2, far, near).wait_send()
+        for chunk in range(chunks):
+            gather_copy(buf, phase, 0, row, far, chunk).wait_send()
+            gather_copy(buf, phase, 1, row, near, chunk).wait_send()
+            gather_copy(buf, phase, 2, far, near, chunk).wait_send()
 
     unit = next(u for u in (16, 12, 8, 6, 4, 3, 2, 1) if cap % u == 0)
 
@@ -245,6 +254,7 @@
         square = split(coup_ref[band])
         squares[band] = dot3(square, square, ROW_DIMS)
 
+    gather_forward(full_ham, 0)
     wait_arrived(ham_send, ham_recv, 0)
     unpack(ham_recv)
     for band in range(bands):
@@ -257,7 +267,6 @@
         spot = slice(part * TW, (part + 1) * TW)
         full_ph[row, spot] = dot3(split(coup_ref[band] * factors), split(total[spot]))
     gather_start(full_ph, 1)
-    gather_forward(full_ham, 0)
     gather_forward(full_ph, 1)
 
     gather_finish(full_ph, 1)
@@ -312,12 +321,18 @@
 
     wait_arrived(back_send, back_recv, 2)
 
-    @pl.loop(0, groups)
-    def _(group):
-        spot = pl.ds(pl.multiple_of(group * TR, TR), TR)
-        for band in range(bands):
-            lanes = slice(band * TW, (band + 1) * TW)
-            total[spot, lanes] += back_recv[back_take_ref[group * bands + band]]
+    block_bands = rows // TW
+
+    def add_back(target):
+        @pl.loop(0, groups // 4)
+        def _(part):
+            for inner in range(4):
+                group = part * 4 + inner
+                spot = pl.ds(pl.multiple_of(group * TR, TR), TR)
+                for index in range(block_bands):
+                    band = target * block_bands + index
+                    lanes = pl.ds(pl.multiple_of(band * TW, TW), TW)
+                    total[spot, lanes] += back_recv[back_take_ref[group * bands + band]]
 
     def turn_copy(target, source):
         return pltpu.make_async_remote_copy(
@@ -332,10 +347,7 @@
     def block_of(target):
         return total[:, pl.ds(pl.multiple_of(target * rows, rows), rows)]
 
-    for target in (far, diagonal_peer, near):
-        turned_send[target] = block_of(target).T
-        turn_copy(target, row).start()
-
+    add_back(row)
     own = block_of(row)
     turned_recv[row] = own.T
     eye_rows = lax.broadcasted_iota(jnp.int32, (rows, rows), 0)
@@ -366,6 +378,11 @@
     for target in (far, diagonal_peer, near):
         rsum_copy(target, row).start()
     for target in (far, diagonal_peer, near):
+        add_back(target)
+        turned_send[target] = block_of(target).T
+        turn_copy(target, row).start()
+
+    for target in (far, diagonal_peer, near):
         rsum_copy(target, target).wait_recv()
     partial_value = row_sums[0]
     for block in range(1, rgroups):
@@ -386,13 +403,13 @@
     def _(step):
         csum_copy(chan_peer(step), me).start()
 
-    for target in (near, far, diagonal_peer):
-        turn_copy(target, target).wait_recv()
-    for block in range(rgroups):
-        for part in range(rows // TW):
-            band = block * (rows // TW) + part
-            lanes = slice(band * TW, (band + 1) * TW)
-            value = total[:, lanes] + turned_recv[block, :, part * TW : (part + 1) * TW]
+    for target in (row, near, far, diagonal_peer):
+        if target is not row:
+            turn_copy(target, target).wait_recv()
+        for part in range(block_bands):
+            band = target * block_bands + part
+            lanes = pl.ds(pl.multiple_of(band * TW, TW), TW)
+            value = total[:, lanes] + turned_recv[target, :, part * TW : (part + 1) * TW]
             comm_ref[:, lanes] = jnp.where(mask_of(band), value, 0.0)
 
     @pl.loop(1, n)
@@ -489,8 +506,8 @@
             dma((3,)),
             dma((3, n)),
             dma((3, n)),
-            dma((2, 3)),
-            dma((2, 3)),
+            dma((2, 3, 4)),
+            dma((2, 3, 4)),
             dma((rgroups,)),
             dma((rgroups,)),
             dma((rgroups,)),
@@ -499,7 +516,7 @@
             dma((n,)),
         ],
         compiler_params=pltpu.CompilerParams(
-            collective_id=0, has_side_effects=True, vmem_limit_bytes=56 * 1024 * 1024
+            collective_id=0, has_side_effects=True, vmem_limit_bytes=42 * 1024 * 1024
         ),
     )(
         eta_pp[0],

time: 144 us -> 141 us (0.979)
  the two profiles are of different devices: /device:TPU:0 before, /device:TPU:19 now
where the time goes in v3:
time: 141 us
  Pallas kernels  132 us (94%)
  local copies, waits for them, and re-layouts  6.58 us (5%)
  between operations  1.98 us (1%)
    pallas_call x1, Pallas kernels, per_device(): pl.pallas_call(functools.partial(kernel, n, cap), out_shape=(jax.ShapeDty...  132 us
    unnamed x18, local copies, waits for them, and re-layouts  6.32 us

profile of v3, /device:TPU:19, one launch (start us, length us, event | category | flops | bytes accessed | tf_op | source)
XLA Modules:
  0.0 141.1 jit_solution(10196298308146127029)
XLA Ops:
  1.9 0.0 copy-start.7
  1.9 0.0 copy-start.6
  2.0 0.6 copy-done.7
  2.6 0.0 copy-done.6
  2.7 0.2 convert_reduce_fusion
  2.9 0.2 select_reduce_fusion
  3.2 0.1 reshape_squeeze.3
  3.2 0.0 copy-start.4
  3.2 0.1 copy.13
  3.3 0.0 copy-start.3
  3.3 0.0 copy-start.5
  3.3 0.1 reshape.42.take_ref
  3.4 0.5 copy-done.4
  3.9 0.1 copy-done.3
  4.0 0.0 copy-done.5
  4.0 0.0 copy-start
  4.0 1.2 copy-done
  5.2 0.0 copy-start.1
  5.2 1.2 copy-done.1
  6.5 0.0 copy-start.2
  6.5 1.0 copy-done.2
  7.5 132.0 %shard_map.113 = (f32[256,1024]{1,0:T(8,128)S(1)}, f32[1,240]{1,0:T(1,128)S(1)}) custom-call(f32[256,1024]{1,0:T(8,128)S(1)} %bitcast.9, f32[256,1024]{1,0:T(8,128)S(1)} %bitcast.10, s32[1]{0:T(128)S(6)} %copy.16.size_ref, f32[1,1024]{1,0:T(1,128)S(1)} %copy-done.3, f32[1,1024]{1,0:T(1,128)S(1)} %copy-done.4, f32[8,128,128]{2,1,0:T(8,128)S(1)} %bitcast.12, ...), custom_call_target="tpu_custom_call" | custom-call | tf_op jit(solution)/shard_map/pallas_call | solution.py:471
  139.5 1.0 copy.18
  140.5 0.6 copy.19
  (6 shorter events, 0.1 us)
Async XLA Ops:
  1.9 0.7 copy-start.7
  1.9 0.7 copy-start.6
  3.2 0.7 copy-start.4
  3.3 0.7 copy-start.3
  3.3 0.7 copy-start.5
  4.0 1.2 copy-start
  5.2 1.2 copy-start.1
  6.5 1.0 copy-start.2
